TPU v7x, 32 devices: a whole 2x2x4 slice. The times are simulated.
32 devices in a mesh: row: 4 (over y, core), col: 8 (over z, x).
Axes of the slice: x: 2, y: 2, z: 4, core: 2. Of those that a mesh axis runs over, the one named last changes fastest.
Arguments:
- block_values: bfloat16 [4, 8, 24, 256, 256], P('row', 'col'), may hold values from -0.078125 to 0.078125
- block_rows: int32 [4, 8, 24], P('row', 'col'), may hold values from 0 to 7, as said below
- block_cols: int32 [4, 8, 24], P('row', 'col'), may hold values from 0 to 7
- block_count: int32 [4, 8], P('row', 'col'), may hold values from 8 to 24, as said below
- basis: bfloat16 [16384, 256], P(('col', 'row')), may hold values from -6 to 6
Outputs:
- sweep_out: float32 [16384, 256], P(('col', 'row'))
Inputs may be any that keep to these rules, and one draw needn't show every extreme that they name: Within one device all slots give distinct (block_rows, block_cols) pairs; slots at or beyond block_count hold no block. `block_count`: some device holds exactly 24 live slots.
All inputs are finite; a program needn't handle non-finite values.
Results may differ from a plain program's by a relative error of at most 0.0026.
Values may be sent and summed in bfloat16 or wider, within the bound.
A program may use at most 64 MiB of HBM per device.

v0:
```python
import jax
import jax.numpy as jnp
from jax import lax
from jax.sharding import PartitionSpec as P

RB = 8
CB = 8


def body(block_values, block_rows, block_cols, block_count, basis):
    blocks = block_values[0, 0]
    row_ids = block_rows[0, 0]
    col_ids = block_cols[0, 0]
    live_count = block_count[0, 0]
    slot_count = blocks.shape[0]
    tile_width = blocks.shape[1]
    live_mask = (jnp.arange(slot_count, dtype=jnp.int32) < live_count).astype(jnp.float32)
    column_basis = lax.all_gather(basis, "row", axis=0, tiled=True)
    masked = jnp.where(live_mask[:, None, None] > 0.5, blocks, jnp.zeros_like(blocks))
    placed = jnp.zeros((RB, tile_width, CB, tile_width), jnp.bfloat16)
    placed = placed.at[row_ids, :, col_ids, :].set(masked)
    matrix = placed.reshape(RB * tile_width, CB * tile_width)
    row_part = jnp.dot(matrix, column_basis, preferred_element_type=jnp.float32)
    row_basis = lax.psum(row_part, "col").astype(jnp.bfloat16)
    column_part = lax.dot_general(
        matrix, row_basis, (((0,), (0,)), ((), ())), preferred_element_type=jnp.float32
    )
    return lax.psum_scatter(column_part, "row", scatter_dimension=0, tiled=True)


def solution(mesh):
    in_specs = (
        P("row", "col", None, None, None),
        P("row", "col", None),
        P("row", "col", None),
        P("row", "col"),
        P(("col", "row"), None),
    )
    out_specs = P(("col", "row"), None)
    return jax.shard_map(body, mesh=mesh, in_specs=in_specs, out_specs=out_specs, check_vma=False)
```

profile of v0, /device:TPU:0, one launch (start us, length us, event | category | flops | bytes accessed | tf_op | source)
XLA Modules:
  0.0 189.7 jit_solution(8094490941906485515)
XLA Ops:
  6.5 0.0 all-gather.2.cloned.1.call-start
  6.5 0.7 all-gather.2.cloned.1.call-update
  7.3 0.0 reduce-scatter.2.cloned.1.call-start
  8.0 0.7 fusion.4
  8.6 2.2 %bitcast_select_fusion = bf16[24,256,256]{2,1,0:T(8,128)(2,1)S(1)} fusion(bf16[1,1,24,256,256]{4,3,2,1,0:T(8,128)(2,1)} %param.5, pred[24]{0:T(512)(128)(4,1)S(1)} %fusion.3), kind=kLoop, calls=%fused_computation.1 | loop fusion | flops 1572864 | bytes 6291480 | tf_op jit(solution)/shard_map/jit(_where)/select_n | solution.py:19
  10.8 4.2 %broadcast_in_dim.17 = bf16[8,256,8,256]{3,1,2,0:T(8,128)(2,1)} broadcast(bf16[]{:T(256)} %constant.4.clone.1), dimensions={} | broadcast | bytes 8388610 | tf_op jit(solution)/shard_map/broadcast_in_dim | solution.py:20
  15.0 7.7 %scatter_fusion = bf16[8,256,8,256]{3,1,2,0:T(8,128)(2,1)} fusion(bf16[8,256,8,256]{3,1,2,0:T(8,128)(2,1)} %broadcast_in_dim.17, s32[24]{0:T(128)S(1)} %fusion.4, bf16[24,256,256]{2,1,0:T(8,128)(2,1)S(1)} %bitcast_select_fusion), kind=kCustom, calls=%fused_computation | custom fusion | bytes 9437376 | tf_op jit(solution)/shard_map/scatter | solution.py:21
  22.8 11.8 %copy.6 = bf16[8,256,8,256]{3,2,1,0:T(8,128)(2,1)} copy(bf16[8,256,8,256]{3,1,2,0:T(8,128)(2,1)} %scatter_fusion) | data formatting | bytes 16777216 | tf_op jit(solution)/shard_map/scatter | solution.py:21
  34.5 10.3 %copy.7 = bf16[256,8,8,256]{3,1,2,0:T(8,128)(2,1)} copy(bf16[256,8,8,256]{3,2,1,0:T(8,128)(2,1)} %bitcast.21) | data formatting | bytes 16777216
  44.8 0.0 all-gather.2.cloned.1.call-done
  44.8 6.0 %fusion.5 = f32[2048,256]{1,0:T(8,128)S(1)} fusion(bf16[2048,2048]{1,0:T(8,128)(2,1)} %bitcast.22, bf16[2048,256]{1,0:T(8,128)(2,1)} %all-gather.2.cloned.1.call-done), kind=kOutput, calls=%fused_computation.13 | convolution fusion | flops 2147483648 | bytes 11534336 | tf_op jit(solution)/shard_map/dot_general | solution.py:23
  50.8 96.2 %all-reduce.1 = bf16[2048,256]{1,0:T(8,128)(2,1)S(1)} all-reduce(f32[2048,256]{1,0:T(8,128)S(1)} %fusion.5), channel_id=1, replica_groups=mesh['row'=4,'col'=8] {'col'}, use_global_device_ids=true, to_apply=%region_1.2 | all-reduce | flops 524288 | bytes 3145728 | tf_op jit(solution)/shard_map/psum | solution.py:24
  147.0 7.2 %fusion.6 = f32[2048,256]{1,0:T(8,128)} fusion(bf16[2048,2048]{1,0:T(8,128)(2,1)} %bitcast.23, bf16[2048,256]{1,0:T(8,128)(2,1)S(1)} %all-reduce.1), kind=kOutput, calls=%fused_computation.14 | convolution fusion | flops 2147483648 | bytes 11534336 | tf_op jit(solution)/shard_map/dot_general | solution.py:25
  154.2 0.0 reduce-scatter.2.cloned.1.call-update
  154.3 28.6 %reduce-scatter.2.cloned.1.call-done = f32[512,256]{1,0:T(8,128)} async-done(((f32[2048,256]{1,0:T(8,128)}), f32[512,256]{1,0:T(8,128)}) %reduce-scatter.2.cloned.1.call-update) | async-done | bytes 524304 | tf_op jit(solution)/shard_map/reduce_scatter | solution.py:28
  (1 shorter events, 0.0 us)
Async XLA Ops:
  6.5 38.3 %all-gather.2.cloned.1.call-start = ((), (), s32[]{:S(2)}) async-start(), calls=%async_computation.1 | async-start | bytes 1310720 | tf_op jit(solution)/shard_map/all_gather | solution.py:18
  7.3 175.6 %reduce-scatter.2.cloned.1.call-start = ((), (), s32[]{:S(2)}) async-start(), calls=%async_computation.2 | async-start | bytes 2621440 | tf_op jit(solution)/shard_map/reduce_scatter | solution.py:28
Sparse Core Ops, SparseCore 0:
  8.9 19.4 all-gather.1
  154.4 28.4 reduce-scatter.1
where the time goes:
time: 190 us
  blocking collectives  96.2 us (51%)
  local copies, waits for them, and re-layouts  34 us (18%)
  waiting for transfers between devices  29.4 us (15%)
  between operations  14.1 us (7%)
  matrix products  13.2 us (7%)
  other arithmetic  2.85 us (2%)
    psum x1, blocking collectives, body(): row_basis = lax.psum(row_part, 'col').astype(jnp.bfloat16)  96.2 us
    reduce_scatter x1, waiting for transfers between devices, body(): return lax.psum_scatter(column_part, 'row', scatter_dimension=0, tiled=True)  28.6 us
    scatter x2, local copies, waits for them, and re-layouts, body(): placed = placed.at[row_ids, :, col_ids, :].set(masked)  19.5 us
    unnamed x1, local copies, waits for them, and re-layouts  10.3 us
    dot_general x1, matrix products, body(): lax.dot_general(matrix, row_basis, (((0,), (0,)), ((), ())), preferred_el...  7.25 us
    dot_general x1, matrix products, body(): row_part = jnp.dot(matrix, column_basis, preferred_element_type=jnp.float32)  5.96 us
    broadcast_in_dim x1, local copies, waits for them, and re-layouts, body(): placed = jnp.zeros((RB, tile_width, CB, tile_width), jnp.bfloat16)  4.24 us
  transfers between devices with their start and end apart: 2, of which 1 were waited for; matrix products, arithmetic and copies ran while one was open for 19% of the time, Pallas kernels for 0%

commit v1 on v0

v1 whole, which is shorter than its diff:
```python
import functools
import math

import jax
import jax.numpy as jnp
from jax import lax
from jax.experimental import pallas as pl
from jax.experimental.pallas import tpu as pltpu
from jax.sharding import PartitionSpec as P

RB = 8
CB = 8
LANES = 128
EXTRA = 16
MESH = pl.DeviceIdType.MESH


def encode(dst, value):
    rows = value.shape[0]
    top = jnp.max(jnp.abs(value), axis=0, keepdims=True)
    power = jnp.floor(jnp.log2(jnp.maximum(top, 1e-30)))
    scaled = jnp.round(value * jnp.exp2(13.9 - power)).astype(jnp.int32)
    dst[pl.ds(0, rows), :] = scaled.astype(jnp.int16)
    tail = jnp.broadcast_to(power.astype(jnp.int32), (EXTRA, value.shape[1]))
    dst[pl.ds(rows, EXTRA), :] = tail.astype(jnp.int16)


def decode(src):
    rows = src.shape[0] - EXTRA
    power = src[pl.ds(rows, EXTRA), :].astype(jnp.int32).astype(jnp.float32)[0:1, :]
    values = src[pl.ds(0, rows), :].astype(jnp.int32).astype(jnp.float32)
    return values * jnp.exp2(power - 13.9)


def kernel(
    NR, NX, NZ,
    table, basis, blocks, out,
    held, turned, matrix, flipped, gathered, part, xs, xr, zs, zr, row_basis, cs, cr, ys, yr,
    load_sem, g_ss, g_sr, x_ss, x_sr, z_ss, z_sr, az_ss, ax_ss, a_sr, c_ss, c_sr, y_ss, y_sr,
):
    NY = NR // 2
    slots, size, _ = blocks.shape
    chunks = gathered.shape[0]
    share = basis.shape[0]
    piece = part.shape[1] // (NX * NZ)
    depth = gathered.shape[1]
    row = lax.axis_index("row")
    col = lax.axis_index("col")
    y, k = row // 2, row % 2
    z, x = col // NX, col % NX
    other = 1 - k

    def dev(y_, k_, z_, x_):
        return (y_ * 2 + k_, z_ * NX + x_)

    def remote(src, dst, send, recv, to):
        return pltpu.make_async_remote_copy(
            src_ref=src, dst_ref=dst, send_sem=send, recv_sem=recv, device_id=to, device_id_type=MESH
        )

    sends = []

    def start(copy, cond=None):
        sends.append((copy, cond))
        if cond is None:
            copy.start()
        else:
            pl.when(cond)(copy.start)

    load = pltpu.make_async_copy(blocks, held.at[pl.ds(0, slots)], load_sem)
    load.start()

    barrier = pltpu.get_barrier_semaphore()

    def greet(to):
        pl.semaphore_signal(barrier, inc=1, device_id=to, device_id_type=MESH)

    greet(dev(y, other, z, x))
    for dy in range(1, NY):
        greet(dev((y + dy) % NY, k, z, x))
    for dx in range(1, NX):
        greet(dev(y, k, z, (x + dx) % NX))
    pl.when(z > 0)(lambda: greet(dev(y, k, z - 1, x)))
    pl.when(z < NZ - 1)(lambda: greet(dev(y, k, z + 1, x)))
    ends = (z + NZ - 1) // NZ + (2 * NZ - 2 - z) // NZ
    pl.semaphore_wait(barrier, NY + NX - 1 + ends)

    def g_rows(r):
        return pl.ds(pl.multiple_of(r * share, share), share)

    def g_dst(h, r):
        return gathered.at[h, g_rows(r)]

    for h in range(chunks):
        src = basis.at[:, pl.ds(h * LANES, LANES)]
        for dy in range(1, NY):
            start(remote(src, g_dst(h, row), g_ss.at[h, dy], g_sr.at[h, row], dev((y + dy) % NY, k, z, x)))
        start(remote(src, g_dst(h, row), g_ss.at[h, 0], g_sr.at[h, row], dev(y, other, z, x)))
        gathered[h, g_rows(row), :] = basis[:, pl.ds(h * LANES, LANES)]

    def await_recv(dst, sem):
        remote(dst, dst, sem, sem, dev(y, other, z, x)).wait_recv()

    def gather(h):
        for dy in range(1, NY):
            r = ((y + dy) % NY) * 2 + k
            await_recv(g_dst(h, r), g_sr.at[h, r])
            start(remote(g_dst(h, r), g_dst(h, r), g_ss.at[h, NY + dy], g_sr.at[h, r], dev(y, other, z, x)))
        for dy in range(NY):
            r = ((y + dy) % NY) * 2 + other
            await_recv(g_dst(h, r), g_sr.at[h, r])

    held[slots] = jnp.zeros((size, size), held.dtype)
    load.wait()

    def lay(i, _):
        for j in range(CB):
            matrix[pl.ds(pl.multiple_of(i * size, size), size), pl.ds(j * size, size)] = held[table[i * CB + j]]
        return 0

    lax.fori_loop(0, RB, lay, 0)

    def turn_all():
        def turn(s, _):
            turned[s] = held[s].T
            return 0

        lax.fori_loop(0, slots + 1, turn, 0)

        def lay_turned(j, _):
            for i in range(RB):
                flipped[pl.ds(pl.multiple_of(j * size, size), size), pl.ds(i * size, size)] = turned[table[i * CB + j]]
            return 0

        lax.fori_loop(0, CB, lay_turned, 0)

    def p_rows(x_, z_):
        return pl.ds(pl.multiple_of((x_ * NZ + z_) * piece, piece), piece)

    def target(e):
        half = (2 * z) // NZ
        sign = 1 - 2 * half
        near = half * (NZ - 1 - z) + (1 - half) * z
        far = (e - 2 * near - 1 + 2 * NZ) // (2 * NZ)
        away = far * (e - near) + (1 - far) * ((e + 1) // 2)
        way = sign * (far + (1 - far) * (1 - 2 * (e % 2)))
        return z + way * away, way

    def product(h, x_, t):
        rows = p_rows(x_, t)
        return jnp.dot(matrix[rows, :], gathered[h], preferred_element_type=jnp.float32)

    def reduce_x(h):
        for dx in range(1, NX):
            x_ = (x + dx) % NX
            for e in range(NZ - 1, -1, -1):
                t, _ = target(e)
                encode(xs.at[h, dx, t], product(h, x_, t))
                start(remote(xs.at[h, dx, t], xr.at[h, dx, t], x_ss.at[h, dx, t], x_sr.at[h, dx, t], dev(y, k, z, x_)))

        def own(t, _):
            part[h, p_rows(x, t), :] = product(h, x, t)
            return 0

        lax.fori_loop(0, NZ, own, 0)

    def reduce_z(h, e):
        t, way = target(e)
        rows = p_rows(x, t)
        total = part[h, rows, :]
        for dx in range(1, NX):
            await_recv(xr.at[h, dx, t], x_sr.at[h, dx, t])
            total = total + decode(xr.at[h, dx, t])

        def add(flow):
            await_recv(zr.at[h, flow, t], z_sr.at[h, flow, t])
            part[h, rows, :] += decode(zr.at[h, flow, t])

        part[h, rows, :] = total
        if e > 0:
            flow = (1 - way) // 2
            back = z - way
            pl.when((back >= 0) & (back < NZ))(lambda: add(flow))
            encode(zs.at[h, t], part[h, rows, :])
            start(remote(zs.at[h, t], zr.at[h, flow, t], z_ss.at[h, t], z_sr.at[h, flow, t], dev(y, k, z + way, x)))
        else:
            pl.when(z > 0)(lambda: add(0))
            pl.when(z < NZ - 1)(lambda: add(1))
            row_basis[h, rows, :] = part[h, rows, :].astype(row_basis.dtype)

    def spread(h, e):
        t, way = target(e)
        q = x * NZ + t
        ref = row_basis.at[h, p_rows(x, t)]
        if e == 0:
            start(remote(ref, ref, az_ss.at[h, 0, t], a_sr.at[h, q], dev(y, k, z + 1, x)), z < NZ - 1)
            start(remote(ref, ref, az_ss.at[h, 1, t], a_sr.at[h, q], dev(y, k, z - 1, x)), z > 0)
        else:
            await_recv(ref, a_sr.at[h, q])
            onward = z - way
            start(
                remote(ref, ref, az_ss.at[h, 0, t], a_sr.at[h, q], dev(y, k, onward, x)),
                (onward >= 0) & (onward < NZ),
            )
        for dx in range(1, NX):
            start(remote(ref, ref, ax_ss.at[h, dx, t], a_sr.at[h, q], dev(y, k, z, (x + dx) % NX)))

    def collect(h):
        for dx in range(1, NX):
            x_ = (x + dx) % NX
            for t in range(NZ):
                await_recv(row_basis.at[h, p_rows(x_, t)], a_sr.at[h, x_ * NZ + t])

    def back_product(h, r):
        rows = g_rows(r)
        return jnp.dot(flipped[rows, :], row_basis[h], preferred_element_type=jnp.float32)

    def back_core(h):
        for dy in list(range(1, NY)) + [0]:
            y_ = (y + dy) % NY
            cs[h, dy] = back_product(h, y_ * 2 + other).astype(cs.dtype)
            start(remote(cs.at[h, dy], cr.at[h, dy], c_ss.at[h, dy], c_sr.at[h, dy], dev(y, other, z, x)))

    def back_y(h):
        for dy in list(range(1, NY)) + [0]:
            y_ = (y + dy) % NY
            total = back_product(h, y_ * 2 + k)
            await_recv(cr.at[h, dy], c_sr.at[h, dy])
            total = total + cr[h, dy].astype(jnp.float32)
            if dy > 0:
                ys[h, dy] = total.astype(ys.dtype)
                start(remote(ys.at[h, dy], yr.at[h, dy], y_ss.at[h, dy], y_sr.at[h, dy], dev(y_, k, z, x)))
            else:
                out[:, pl.ds(h * LANES, LANES)] = total

    def finish(h):
        total = out[:, pl.ds(h * LANES, LANES)]
        for dy in range(1, NY):
            await_recv(yr.at[h, dy], y_sr.at[h, dy])
            total = total + yr[h, dy].astype(jnp.float32)
        out[:, pl.ds(h * LANES, LANES)] = total

    gather(0)
    reduce_x(0)
    for h in range(1, chunks):
        gather(h)
        reduce_x(h)
    turn_all()
    for e in range(NZ - 1, -1, -1):
        reduce_z(0, e)
    for h in range(chunks):
        for e in range(NZ):
            spread(h, e)
            if h + 1 < chunks:
                reduce_z(h + 1, NZ - 1 - e)
    for h in range(chunks):
        collect(h)
        back_core(h)
        back_y(h)
    for h in range(chunks):
        finish(h)
    for copy, cond in sends:
        if cond is None:
            copy.wait_send()
        else:
            pl.when(cond)(copy.wait_send)


def body(NR, NC, block_values, block_rows, block_cols, block_count, basis):
    blocks = block_values[0, 0]
    slots, size, _ = blocks.shape
    share, rank = basis.shape
    NX = math.isqrt(max(NC // 2, 1))
    if NC % NX:
        NX = 1
    NZ = NC // NX
    NY = NR // 2
    chunks = rank // LANES
    piece = RB * size // NC
    places = jnp.where(
        jnp.arange(slots, dtype=jnp.int32) < block_count[0, 0], block_rows[0, 0] * CB + block_cols[0, 0], -1
    )
    hit = places[None, :] == jnp.arange(RB * CB, dtype=jnp.int32)[:, None]
    table = jnp.min(jnp.where(hit, jnp.arange(slots, dtype=jnp.int32)[None, :], slots), axis=1)
    bf16, i16 = jnp.bfloat16, jnp.int16
    DMA = pltpu.SemaphoreType.DMA
    V = pltpu.VMEM
    return pl.pallas_call(
        functools.partial(kernel, NR, NX, NZ),
        out_shape=jax.ShapeDtypeStruct((share, rank), jnp.float32),
        in_specs=[
            pl.BlockSpec(memory_space=pltpu.SMEM),
            pl.BlockSpec(memory_space=pltpu.VMEM),
            pl.BlockSpec(memory_space=pl.ANY),
        ],
        out_specs=pl.BlockSpec(memory_space=pltpu.VMEM),
        scratch_shapes=[
            V((slots + 1, size, size), bf16),
            V((slots + 1, size, size), bf16),
            V((RB * size, CB * size), bf16),
            V((CB * size, RB * size), bf16),
            V((chunks, CB * size, LANES), bf16),
            V((chunks, RB * size, LANES), jnp.float32),
            V((chunks, NX, NZ, piece + EXTRA, LANES), i16),
            V((chunks, NX, NZ, piece + EXTRA, LANES), i16),
            V((chunks, NZ, piece + EXTRA, LANES), i16),
            V((chunks, 2, NZ, piece + EXTRA, LANES), i16),
            V((chunks, RB * size, LANES), bf16),
            V((chunks, NY, share, LANES), bf16),
            V((chunks, NY, share, LANES), bf16),
            V((chunks, NY, share, LANES), bf16),
            V((chunks, NY, share, LANES), bf16),
            DMA,
            DMA((chunks, 2 * NY)),
            DMA((chunks, NR)),
            DMA((chunks, NX, NZ)),
            DMA((chunks, NX, NZ)),
            DMA((chunks, NZ)),
            DMA((chunks, 2, NZ)),
            DMA((chunks, 2, NZ)),
            DMA((chunks, NX, NZ)),
            DMA((chunks, NC)),
            DMA((chunks, NY)),
            DMA((chunks, NY)),
            DMA((chunks, NY)),
            DMA((chunks, NY)),
        ],
        compiler_params=pltpu.CompilerParams(
            collective_id=0, has_side_effects=True, vmem_limit_bytes=56 * 1024 * 1024
        ),
    )(table, basis, blocks)


def solution(mesh):
    in_specs = (
        P("row", "col", None, None, None),
        P("row", "col", None),
        P("row", "col", None),
        P("row", "col"),
        P(("col", "row"), None),
    )
    out_specs = P(("col", "row"), None)
    run = functools.partial(body, mesh.shape["row"], mesh.shape["col"])
    return jax.shard_map(run, mesh=mesh, in_specs=in_specs, out_specs=out_specs, check_vma=False)
```

time: 190 us -> 76.7 us (0.40)
  blocking collectives: 96.2 us -> 0 us
  Pallas kernels: 0 us -> 72.7 us
  local copies, waits for them, and re-layouts: 34 us -> 1.87 us
  waiting for transfers between devices: 29.4 us -> 0 us
  between operations: 14.1 us -> 0.66 us
  matrix products: 13.2 us -> 0 us
    psum x1 -> x0, blocking collectives: 96.2 us -> none  [body(): row_basis = lax.psum(row_part, 'col').astype(jnp.bfloat16)]
    pallas_call x0 -> x1, Pallas kernels: none -> 72.7 us  [body(): pl.pallas_call(functools.partial(kernel, NR, NX, NZ), out_shape=jax.Shape...]
    reduce_scatter x1 -> x0, waiting for transfers between devices: 28.6 us -> none  [body(): return lax.psum_scatter(column_part, 'row', scatter_dimension=0, tiled=True)]
    scatter x2 -> x0, local copies, waits for them, and re-layouts: 19.5 us -> none  [body(): placed = placed.at[row_ids, :, col_ids, :].set(masked)]
    dot_general x2 -> x0, matrix products: 13.2 us -> none  [the longest x1 7.25 us: body(): lax.dot_general(matrix, row_basis, (((0,), (0,)), ((), ())), preferred_el...]
    unnamed x1, local copies, waits for them, and re-layouts: 10.3 us -> 1.87 us
    broadcast_in_dim x1 -> x0, local copies, waits for them, and re-layouts: 4.24 us -> none  [body(): placed = jnp.zeros((RB, tile_width, CB, tile_width), jnp.bfloat16)]
  transfers between devices with their start and end apart: 2 -> 0, of which waited for: 1 -> 0; matrix products, arithmetic and copies ran while one was open for 19% -> 0% of each run, Pallas kernels for 0% -> 0%
where the time goes in v1:
time: 76.7 us; the launch traced here: 76.5 us
  Pallas kernels  72.7 us (95%)
  local copies, waits for them, and re-layouts  1.87 us (2%)
  other arithmetic  1.28 us (2%)
    pallas_call x1, Pallas kernels, body(): pl.pallas_call(functools.partial(kernel, NR, NX, NZ), out_shape=jax.Shape...  72.7 us
    unnamed x1, local copies, waits for them, and re-layouts  1.87 us

profile of v1, /device:TPU:0, one launch (start us, length us, event | category | flops | bytes accessed | tf_op | source)
XLA Modules:
  0.0 76.5 jit_solution(7522448468848622100)
XLA Ops:
  0.7 0.7 compare_select_fusion
  1.3 0.6 select_reduce_fusion.table
  1.9 72.7 %shard_map.55 = f32[512,256]{1,0:T(8,128)} custom-call(s32[64]{0:T(128)} %select_reduce_fusion.table, bf16[512,256]{1,0:T(8,128)(2,1)} %basis.1, bf16[24,256,256]{2,1,0:T(8,128)(2,1)} %bitcast.5), custom_call_target="tpu_custom_call" | custom-call | tf_op jit(solution)/shard_map/pallas_call | solution.py:288
  74.6 1.9 %copy.8 = f32[512,256]{1,0:T(8,128)} copy(f32[512,256]{1,0:T(8,128)} %shard_map.55) | data formatting | bytes 1048576

commit v2 on v1

--- a/solution.py
+++ b/solution.py
@@ -60,12 +60,9 @@
 
     sends = []
 
-    def start(copy, cond=None):
-        sends.append((copy, cond))
-        if cond is None:
-            copy.start()
-        else:
-            pl.when(cond)(copy.start)
+    def start(copy):
+        sends.append(copy)
+        copy.start()
 
     load = pltpu.make_async_copy(blocks, held.at[pl.ds(0, slots)], load_sem)
     load.start()
@@ -80,10 +77,9 @@
         greet(dev((y + dy) % NY, k, z, x))
     for dx in range(1, NX):
         greet(dev(y, k, z, (x + dx) % NX))
-    pl.when(z > 0)(lambda: greet(dev(y, k, z - 1, x)))
-    pl.when(z < NZ - 1)(lambda: greet(dev(y, k, z + 1, x)))
-    ends = (z + NZ - 1) // NZ + (2 * NZ - 2 - z) // NZ
-    pl.semaphore_wait(barrier, NY + NX - 1 + ends)
+    for dz in range(1, NZ):
+        greet(dev(y, k, (z + dz) % NZ, x))
+    pl.semaphore_wait(barrier, NY + NX + NZ - 2)
 
     def g_rows(r):
         return pl.ds(pl.multiple_of(r * share, share), share)
@@ -137,73 +133,61 @@
     def p_rows(x_, z_):
         return pl.ds(pl.multiple_of((x_ * NZ + z_) * piece, piece), piece)
 
-    def target(e):
-        half = (2 * z) // NZ
-        sign = 1 - 2 * half
-        near = half * (NZ - 1 - z) + (1 - half) * z
-        far = (e - 2 * near - 1 + 2 * NZ) // (2 * NZ)
-        away = far * (e - near) + (1 - far) * ((e + 1) // 2)
-        way = sign * (far + (1 - far) * (1 - 2 * (e % 2)))
-        return z + way * away, way
-
-    def product(h, x_, t):
-        rows = p_rows(x_, t)
-        return jnp.dot(matrix[rows, :], gathered[h], preferred_element_type=jnp.float32)
+    def x_rows(x_):
+        return pl.ds(pl.multiple_of(x_ * NZ * piece, NZ * piece), NZ * piece)
+
+    def product(h, x_):
+        part[h, x_rows(x_), :] = jnp.dot(matrix[x_rows(x_), :], gathered[h], preferred_element_type=jnp.float32)
+
+    z_order = [(z + dz) % NZ for dz in range(1, NZ)]
 
     def reduce_x(h):
         for dx in range(1, NX):
             x_ = (x + dx) % NX
-            for e in range(NZ - 1, -1, -1):
-                t, _ = target(e)
-                encode(xs.at[h, dx, t], product(h, x_, t))
+            product(h, x_)
+            for t in z_order + [z]:
+                encode(xs.at[h, dx, t], part[h, p_rows(x_, t), :])
                 start(remote(xs.at[h, dx, t], xr.at[h, dx, t], x_ss.at[h, dx, t], x_sr.at[h, dx, t], dev(y, k, z, x_)))
-
-        def own(t, _):
-            part[h, p_rows(x, t), :] = product(h, x, t)
-            return 0
-
-        lax.fori_loop(0, NZ, own, 0)
-
-    def reduce_z(h, e):
-        t, way = target(e)
-        rows = p_rows(x, t)
-        total = part[h, rows, :]
+        product(h, x)
+
+    def add_x(h, t):
+        total = part[h, p_rows(x, t), :]
         for dx in range(1, NX):
             await_recv(xr.at[h, dx, t], x_sr.at[h, dx, t])
             total = total + decode(xr.at[h, dx, t])
-
-        def add(flow):
-            await_recv(zr.at[h, flow, t], z_sr.at[h, flow, t])
-            part[h, rows, :] += decode(zr.at[h, flow, t])
-
-        part[h, rows, :] = total
-        if e > 0:
-            flow = (1 - way) // 2
-            back = z - way
-            pl.when((back >= 0) & (back < NZ))(lambda: add(flow))
-            encode(zs.at[h, t], part[h, rows, :])
-            start(remote(zs.at[h, t], zr.at[h, flow, t], z_ss.at[h, t], z_sr.at[h, flow, t], dev(y, k, z + way, x)))
-        else:
-            pl.when(z > 0)(lambda: add(0))
-            pl.when(z < NZ - 1)(lambda: add(1))
-            row_basis[h, rows, :] = part[h, rows, :].astype(row_basis.dtype)
-
-    def spread(h, e):
-        t, way = target(e)
-        q = x * NZ + t
+        return total
+
+    def reduce_z(h):
+        for dz, t in enumerate(z_order, 1):
+            encode(zs.at[h, dz], add_x(h, t))
+            start(remote(zs.at[h, dz], zr.at[h, dz], z_ss.at[h, dz], z_sr.at[h, dz], dev(y, k, t, x)))
+
+    def pass_x(h, t):
         ref = row_basis.at[h, p_rows(x, t)]
-        if e == 0:
-            start(remote(ref, ref, az_ss.at[h, 0, t], a_sr.at[h, q], dev(y, k, z + 1, x)), z < NZ - 1)
-            start(remote(ref, ref, az_ss.at[h, 1, t], a_sr.at[h, q], dev(y, k, z - 1, x)), z > 0)
-        else:
-            await_recv(ref, a_sr.at[h, q])
-            onward = z - way
-            start(
-                remote(ref, ref, az_ss.at[h, 0, t], a_sr.at[h, q], dev(y, k, onward, x)),
-                (onward >= 0) & (onward < NZ),
-            )
-        for dx in range(1, NX):
-            start(remote(ref, ref, ax_ss.at[h, dx, t], a_sr.at[h, q], dev(y, k, z, (x + dx) % NX)))
+        for dx in range(1, NX):
+            start(remote(ref, ref, ax_ss.at[h, dx, t], a_sr.at[h, x * NZ + t], dev(y, k, z, (x + dx) % NX)))
+
+    def settle(h):
+        total = add_x(h, z)
+        for dz in range(1, NZ):
+            await_recv(zr.at[h, dz], z_sr.at[h, dz])
+            total = total + decode(zr.at[h, dz])
+        row_basis[h, p_rows(x, z), :] = total.astype(row_basis.dtype)
+        ref = row_basis.at[h, p_rows(x, z)]
+        for dz, t in enumerate(z_order, 1):
+            start(remote(ref, ref, az_ss.at[h, dz], a_sr.at[h, x * NZ + z], dev(y, k, t, x)))
+        pass_x(h, z)
+
+    def spread(h):
+        for t in z_order:
+            await_recv(row_basis.at[h, p_rows(x, t)], a_sr.at[h, x * NZ + t])
+            pass_x(h, t)
+
+    def back_half(h, x_):
+        return jnp.dot(flipped[:, x_rows(x_)], row_basis[h, x_rows(x_), :], preferred_element_type=jnp.float32)
+
+    def back_own(h):
+        part[h] = back_half(h, x)
 
     def collect(h):
         for dx in range(1, NX):
@@ -213,7 +197,13 @@
 
     def back_product(h, r):
         rows = g_rows(r)
-        return jnp.dot(flipped[rows, :], row_basis[h], preferred_element_type=jnp.float32)
+        total = part[h, rows, :]
+        for dx in range(1, NX):
+            x_ = (x + dx) % NX
+            total = total + jnp.dot(
+                flipped[rows, x_rows(x_)], row_basis[h, x_rows(x_), :], preferred_element_type=jnp.float32
+            )
+        return total
 
     def back_core(h):
         for dy in list(range(1, NY)) + [0]:
@@ -246,24 +236,24 @@
         gather(h)
         reduce_x(h)
     turn_all()
-    for e in range(NZ - 1, -1, -1):
-        reduce_z(0, e)
     for h in range(chunks):
-        for e in range(NZ):
-            spread(h, e)
-            if h + 1 < chunks:
-                reduce_z(h + 1, NZ - 1 - e)
+        reduce_z(h)
+        if h > 0:
+            spread(h - 1)
+        settle(h)
+        if h > 0:
+            back_own(h - 1)
+    spread(chunks - 1)
     for h in range(chunks):
         collect(h)
         back_core(h)
         back_y(h)
+        if h + 1 == chunks - 1:
+            back_own(h + 1)
     for h in range(chunks):
         finish(h)
-    for copy, cond in sends:
-        if cond is None:
-            copy.wait_send()
-        else:
-            pl.when(cond)(copy.wait_send)
+    for copy in sends:
+        copy.wait_send()
 
 
 def body(NR, NC, block_values, block_rows, block_cols, block_count, basis):
@@ -304,7 +294,7 @@
             V((chunks, NX, NZ, piece + EXTRA, LANES), i16),
             V((chunks, NX, NZ, piece + EXTRA, LANES), i16),
             V((chunks, NZ, piece + EXTRA, LANES), i16),
-            V((chunks, 2, NZ, piece + EXTRA, LANES), i16),
+            V((chunks, NZ, piece + EXTRA, LANES), i16),
             V((chunks, RB * size, LANES), bf16),
             V((chunks, NY, share, LANES), bf16),
             V((chunks, NY, share, LANES), bf16),
@@ -316,8 +306,8 @@
             DMA((chunks, NX, NZ)),
             DMA((chunks, NX, NZ)),
             DMA((chunks, NZ)),
-            DMA((chunks, 2, NZ)),
-            DMA((chunks, 2, NZ)),
+            DMA((chunks, NZ)),
+            DMA((chunks, NZ)),
             DMA((chunks, NX, NZ)),
             DMA((chunks, NC)),
             DMA((chunks, NY)),

time: 76.7 us -> 70.5 us (0.919); the launches traced: 76.5 us -> 69.2 us
  Pallas kernels: 72.7 us -> 65.4 us
    pallas_call x1, Pallas kernels: 72.7 us -> 65.4 us  [body(): pl.pallas_call(functools.partial(kernel, NR, NX, NZ), out_shape=jax.Shape...]
where the time goes in v2:
time: 70.5 us; the launch traced here: 69.2 us
  Pallas kernels  65.4 us (93%)
  local copies, waits for them, and re-layouts  1.87 us (3%)
  other arithmetic  1.28 us (2%)
    pallas_call x1, Pallas kernels, body(): pl.pallas_call(functools.partial(kernel, NR, NX, NZ), out_shape=jax.Shape...  65.4 us
    unnamed x1, local copies, waits for them, and re-layouts  1.87 us

profile of v2, /device:TPU:0, one launch (start us, length us, event | category | flops | bytes accessed | tf_op | source)
XLA Modules:
  0.0 69.2 jit_solution(17943557553682834037)
XLA Ops:
  0.7 0.7 compare_select_fusion
  1.3 0.6 select_reduce_fusion.table
  1.9 65.4 %shard_map.55 = f32[512,256]{1,0:T(8,128)} custom-call(s32[64]{0:T(128)} %select_reduce_fusion.table, bf16[512,256]{1,0:T(8,128)(2,1)} %basis.1, bf16[24,256,256]{2,1,0:T(8,128)(2,1)} %bitcast.5), custom_call_target="tpu_custom_call" | custom-call | tf_op jit(solution)/shard_map/pallas_call | solution.py:278
  67.4 1.9 %copy.8 = f32[512,256]{1,0:T(8,128)} copy(f32[512,256]{1,0:T(8,128)} %shard_map.55) | data formatting | bytes 1048576

commit v3 on v2

--- a/solution.py
+++ b/solution.py
@@ -148,7 +148,6 @@
             for t in z_order + [z]:
                 encode(xs.at[h, dx, t], part[h, p_rows(x_, t), :])
                 start(remote(xs.at[h, dx, t], xr.at[h, dx, t], x_ss.at[h, dx, t], x_sr.at[h, dx, t], dev(y, k, z, x_)))
-        product(h, x)
 
     def add_x(h, t):
         total = part[h, p_rows(x, t), :]
@@ -230,26 +229,33 @@
             total = total + yr[h, dy].astype(jnp.float32)
         out[:, pl.ds(h * LANES, LANES)] = total
 
+    turn_all()
     gather(0)
     reduce_x(0)
+    product(0, x)
     for h in range(1, chunks):
         gather(h)
         reduce_x(h)
-    turn_all()
+        reduce_z(h - 1)
+        product(h, x)
+        settle(h - 1)
+        if h > 1:
+            spread(h - 2)
+            back_own(h - 2)
+    last = chunks - 1
+    reduce_z(last)
+    if last > 0:
+        spread(last - 1)
+    settle(last)
+    if last > 0:
+        back_own(last - 1)
+    spread(last)
     for h in range(chunks):
-        reduce_z(h)
-        if h > 0:
-            spread(h - 1)
-        settle(h)
-        if h > 0:
-            back_own(h - 1)
-    spread(chunks - 1)
-    for h in range(chunks):
+        if h == last:
+            back_own(h)
         collect(h)
         back_core(h)
         back_y(h)
-        if h + 1 == chunks - 1:
-            back_own(h + 1)
     for h in range(chunks):
         finish(h)
     for copy in sends:

time: 70.5 us -> 64.9 us (0.921); the launches traced: 69.2 us -> 64.7 us
  Pallas kernels: 65.4 us -> 60.9 us
    pallas_call x1, Pallas kernels: 65.4 us -> 60.9 us  [body(): pl.pallas_call(functools.partial(kernel, NR, NX, NZ), out_shape=jax.Shape...]
where the time goes in v3:
time: 64.9 us; the launch traced here: 64.7 us
  Pallas kernels  60.9 us (94%)
  local copies, waits for them, and re-layouts  1.87 us (3%)
  other arithmetic  1.28 us (2%)
  between operations  0.66 us (1%)
    pallas_call x1, Pallas kernels, body(): pl.pallas_call(functools.partial(kernel, NR, NX, NZ), out_shape=jax.Shape...  60.9 us
    unnamed x1, local copies, waits for them, and re-layouts  1.87 us

profile of v3, /device:TPU:0, one launch (start us, length us, event | category | flops | bytes accessed | tf_op | source)
XLA Modules:
  0.0 64.7 jit_solution(2513011438267423390)
XLA Ops:
  0.7 0.7 %compare_select_fusion = s32[24]{0:T(128)S(1)} fusion(s32[1,1,24]{2,1,0:T(1,128)} %param.7, s32[1,1,24]{2,1,0:T(1,128)} %param.6, s32[]{:T(128)} %bitcast.4), kind=kLoop, calls=%fused_computation.2 | loop fusion | flops 96 | bytes 292 | tf_op jit(solution)/shard_map/jit(_where)/select_n | solution.py:276
  1.3 0.6 select_reduce_fusion.table
  1.9 60.9 %shard_map.55 = f32[512,256]{1,0:T(8,128)} custom-call(s32[64]{0:T(128)} %select_reduce_fusion.table, bf16[512,256]{1,0:T(8,128)(2,1)} %basis.1, bf16[24,256,256]{2,1,0:T(8,128)(2,1)} %bitcast.5), custom_call_target="tpu_custom_call" | custom-call | tf_op jit(solution)/shard_map/pallas_call | solution.py:284
  62.8 1.9 %copy.8 = f32[512,256]{1,0:T(8,128)} copy(f32[512,256]{1,0:T(8,128)} %shard_map.55) | data formatting | bytes 1048576

commit v4 on v3

--- a/solution.py
+++ b/solution.py
@@ -40,10 +40,9 @@
 ):
     NY = NR // 2
     slots, size, _ = blocks.shape
-    chunks = gathered.shape[0]
+    chunks = part.shape[0]
     share = basis.shape[0]
     piece = part.shape[1] // (NX * NZ)
-    depth = gathered.shape[1]
     row = lax.axis_index("row")
     col = lax.axis_index("col")
     y, k = row // 2, row % 2
@@ -85,14 +84,15 @@
         return pl.ds(pl.multiple_of(r * share, share), share)
 
     def g_dst(h, r):
-        return gathered.at[h, g_rows(r)]
+        return gathered.at[g_rows(r), pl.ds(h * LANES, LANES)]
 
     for h in range(chunks):
         src = basis.at[:, pl.ds(h * LANES, LANES)]
         for dy in range(1, NY):
             start(remote(src, g_dst(h, row), g_ss.at[h, dy], g_sr.at[h, row], dev((y + dy) % NY, k, z, x)))
         start(remote(src, g_dst(h, row), g_ss.at[h, 0], g_sr.at[h, row], dev(y, other, z, x)))
-        gathered[h, g_rows(row), :] = basis[:, pl.ds(h * LANES, LANES)]
+
+    gathered[g_rows(row), :] = basis[...]
 
     def await_recv(dst, sem):
         remote(dst, dst, sem, sem, dev(y, other, z, x)).wait_recv()
@@ -102,6 +102,8 @@
             r = ((y + dy) % NY) * 2 + k
             await_recv(g_dst(h, r), g_sr.at[h, r])
             start(remote(g_dst(h, r), g_dst(h, r), g_ss.at[h, NY + dy], g_sr.at[h, r], dev(y, other, z, x)))
+
+    def gather_rest(h):
         for dy in range(NY):
             r = ((y + dy) % NY) * 2 + other
             await_recv(g_dst(h, r), g_sr.at[h, r])
@@ -123,6 +125,7 @@
 
         lax.fori_loop(0, slots + 1, turn, 0)
 
+    def lay_all():
         def lay_turned(j, _):
             for i in range(RB):
                 flipped[pl.ds(pl.multiple_of(j * size, size), size), pl.ds(i * size, size)] = turned[table[i * CB + j]]
@@ -136,15 +139,17 @@
     def x_rows(x_):
         return pl.ds(pl.multiple_of(x_ * NZ * piece, NZ * piece), NZ * piece)
 
-    def product(h, x_):
-        part[h, x_rows(x_), :] = jnp.dot(matrix[x_rows(x_), :], gathered[h], preferred_element_type=jnp.float32)
+    def product(x_):
+        rows = x_rows(x_)
+        result = jnp.dot(matrix[rows, :], gathered[...], preferred_element_type=jnp.float32)
+        for h in range(chunks):
+            part[h, rows, :] = result[:, h * LANES : (h + 1) * LANES]
 
     z_order = [(z + dz) % NZ for dz in range(1, NZ)]
 
     def reduce_x(h):
         for dx in range(1, NX):
             x_ = (x + dx) % NX
-            product(h, x_)
             for t in z_order + [z]:
                 encode(xs.at[h, dx, t], part[h, p_rows(x_, t), :])
                 start(remote(xs.at[h, dx, t], xr.at[h, dx, t], x_ss.at[h, dx, t], x_sr.at[h, dx, t], dev(y, k, z, x_)))
@@ -230,18 +235,25 @@
         out[:, pl.ds(h * LANES, LANES)] = total
 
     turn_all()
-    gather(0)
-    reduce_x(0)
-    product(0, x)
-    for h in range(1, chunks):
+    for h in range(chunks):
         gather(h)
+    for h in range(chunks):
+        gather_rest(h)
+    for dx in range(1, NX):
+        product((x + dx) % NX)
+    for h in range(chunks):
         reduce_x(h)
-        reduce_z(h - 1)
-        product(h, x)
-        settle(h - 1)
-        if h > 1:
-            spread(h - 2)
-            back_own(h - 2)
+    product(x)
+    for h in range(chunks - 1):
+        reduce_z(h)
+        if h == 0:
+            lay_all()
+        settle(h)
+        if h > 0:
+            spread(h - 1)
+            back_own(h - 1)
+    if chunks == 1:
+        lay_all()
     last = chunks - 1
     reduce_z(last)
     if last > 0:
@@ -295,7 +307,7 @@
             V((slots + 1, size, size), bf16),
             V((RB * size, CB * size), bf16),
             V((CB * size, RB * size), bf16),
-            V((chunks, CB * size, LANES), bf16),
+            V((CB * size, rank), bf16),
             V((chunks, RB * size, LANES), jnp.float32),
             V((chunks, NX, NZ, piece + EXTRA, LANES), i16),
             V((chunks, NX, NZ, piece + EXTRA, LANES), i16),

time: 64.9 us -> 64.9 us (level)
  no operation moved by 1% of the time
where the time goes in v4:
time: 64.9 us; the launch traced here: 64.7 us
  Pallas kernels  60.9 us (94%)
  local copies, waits for them, and re-layouts  1.87 us (3%)
  other arithmetic  1.28 us (2%)
  between operations  0.66 us (1%)
    pallas_call x1, Pallas kernels, body(): pl.pallas_call(functools.partial(kernel, NR, NX, NZ), out_shape=jax.Shape...  60.9 us
    unnamed x1, local copies, waits for them, and re-layouts  1.87 us

profile of v4, /device:TPU:0, one launch (start us, length us, event | category | flops | bytes accessed | tf_op | source)
XLA Modules:
  0.0 64.7 jit_solution(15562921177713947071)
XLA Ops:
  0.7 0.7 %compare_select_fusion = s32[24]{0:T(128)S(1)} fusion(s32[1,1,24]{2,1,0:T(1,128)} %param.7, s32[1,1,24]{2,1,0:T(1,128)} %param.6, s32[]{:T(128)} %bitcast.4), kind=kLoop, calls=%fused_computation.2 | loop fusion | flops 96 | bytes 292 | tf_op jit(solution)/shard_map/jit(_where)/select_n | solution.py:288
  1.3 0.6 select_reduce_fusion.table
  1.9 60.9 %shard_map.55 = f32[512,256]{1,0:T(8,128)} custom-call(s32[64]{0:T(128)} %select_reduce_fusion.table, bf16[512,256]{1,0:T(8,128)(2,1)} %basis.1, bf16[24,256,256]{2,1,0:T(8,128)(2,1)} %bitcast.5), custom_call_target="tpu_custom_call" | custom-call | tf_op jit(solution)/shard_map/pallas_call | solution.py:296
  62.8 1.9 %copy.8 = f32[512,256]{1,0:T(8,128)} copy(f32[512,256]{1,0:T(8,128)} %shard_map.55) | data formatting | bytes 1048576

commit v5 on v4

--- a/solution.py
+++ b/solution.py
@@ -145,12 +145,16 @@
         for h in range(chunks):
             part[h, rows, :] = result[:, h * LANES : (h + 1) * LANES]
 
-    z_order = [(z + dz) % NZ for dz in range(1, NZ)]
+    pairs = NZ // 2
+    near = z + 1 - 2 * (z % 2)
+    near_like = [(near + 2 * j) % NZ for j in range(pairs)]
+    alike = [(z + 2 * j) % NZ for j in range(pairs)]
+    z_order = near_like + alike[1:] + [z]
 
     def reduce_x(h):
         for dx in range(1, NX):
             x_ = (x + dx) % NX
-            for t in z_order + [z]:
+            for t in z_order:
                 encode(xs.at[h, dx, t], part[h, p_rows(x_, t), :])
                 start(remote(xs.at[h, dx, t], xr.at[h, dx, t], x_ss.at[h, dx, t], x_sr.at[h, dx, t], dev(y, k, z, x_)))
 
@@ -161,10 +165,21 @@
             total = total + decode(xr.at[h, dx, t])
         return total
 
-    def reduce_z(h):
-        for dz, t in enumerate(z_order, 1):
-            encode(zs.at[h, dz], add_x(h, t))
-            start(remote(zs.at[h, dz], zr.at[h, dz], z_ss.at[h, dz], z_sr.at[h, dz], dev(y, k, t, x)))
+    def send_z(h, slot, value, to):
+        encode(zs.at[h, slot], value)
+        start(remote(zs.at[h, slot], zr.at[h, slot], z_ss.at[h, slot], z_sr.at[h, slot], dev(y, k, to, x)))
+
+    def take_z(h, slot):
+        await_recv(zr.at[h, slot], z_sr.at[h, slot])
+        return decode(zr.at[h, slot])
+
+    def reduce_near(h):
+        for j in range(pairs):
+            send_z(h, j, add_x(h, near_like[j]), near)
+
+    def reduce_far(h):
+        for j in range(1, pairs):
+            send_z(h, pairs + j, add_x(h, alike[j]) + take_z(h, j), alike[j])
 
     def pass_x(h, t):
         ref = row_basis.at[h, p_rows(x, t)]
@@ -172,20 +187,31 @@
             start(remote(ref, ref, ax_ss.at[h, dx, t], a_sr.at[h, x * NZ + t], dev(y, k, z, (x + dx) % NX)))
 
     def settle(h):
-        total = add_x(h, z)
-        for dz in range(1, NZ):
-            await_recv(zr.at[h, dz], z_sr.at[h, dz])
-            total = total + decode(zr.at[h, dz])
+        total = add_x(h, z) + take_z(h, 0)
+        for j in range(1, pairs):
+            total = total + take_z(h, pairs + j)
         row_basis[h, p_rows(x, z), :] = total.astype(row_basis.dtype)
-        ref = row_basis.at[h, p_rows(x, z)]
-        for dz, t in enumerate(z_order, 1):
-            start(remote(ref, ref, az_ss.at[h, dz], a_sr.at[h, x * NZ + z], dev(y, k, t, x)))
+        for j in range(1, pairs):
+            pass_z(h, z, j, alike[j])
+        pass_z(h, z, 0, near)
         pass_x(h, z)
 
-    def spread(h):
-        for t in z_order:
-            await_recv(row_basis.at[h, p_rows(x, t)], a_sr.at[h, x * NZ + t])
-            pass_x(h, t)
+    def pass_z(h, t, slot, to):
+        ref = row_basis.at[h, p_rows(x, t)]
+        start(remote(ref, ref, az_ss.at[h, slot], a_sr.at[h, x * NZ + t], dev(y, k, to, x)))
+
+    def arrived(h, t):
+        await_recv(row_basis.at[h, p_rows(x, t)], a_sr.at[h, x * NZ + t])
+
+    def spread_far(h):
+        for j in range(1, pairs):
+            arrived(h, alike[j])
+            pass_z(h, alike[j], pairs + j, near)
+            pass_x(h, alike[j])
+
+    def spread_near(h, j):
+        arrived(h, near_like[j])
+        pass_x(h, near_like[j])
 
     def back_half(h, x_):
         return jnp.dot(flipped[:, x_rows(x_)], row_basis[h, x_rows(x_), :], preferred_element_type=jnp.float32)
@@ -244,30 +270,33 @@
     for h in range(chunks):
         reduce_x(h)
     product(x)
-    for h in range(chunks - 1):
-        reduce_z(h)
+    for h in range(chunks):
+        reduce_near(h)
         if h == 0:
             lay_all()
+        else:
+            spread_far(h - 1)
+        reduce_far(h)
+        if h > 0:
+            for j in range(pairs):
+                spread_near(h - 1, j)
         settle(h)
         if h > 0:
-            spread(h - 1)
             back_own(h - 1)
-    if chunks == 1:
-        lay_all()
     last = chunks - 1
-    reduce_z(last)
-    if last > 0:
-        spread(last - 1)
-    settle(last)
-    if last > 0:
-        back_own(last - 1)
-    spread(last)
-    for h in range(chunks):
-        if h == last:
-            back_own(h)
+    spread_far(last)
+    spread_near(last, 0)
+    for h in range(last):
         collect(h)
         back_core(h)
+    for j in range(1, pairs):
+        spread_near(last, j)
+    for h in range(last):
         back_y(h)
+    back_own(last)
+    collect(last)
+    back_core(last)
+    back_y(last)
     for h in range(chunks):
         finish(h)
     for copy in sends:

time: 64.9 us -> 66.4 us (1.023)
  Pallas kernels: 60.9 us -> 62.4 us
    pallas_call x1, Pallas kernels: 60.9 us -> 62.4 us  [body(): pl.pallas_call(functools.partial(kernel, NR, NX, NZ), out_shape=jax.Shape...]
where the time goes in v5:
time: 66.4 us; the launch traced here: 66.2 us
  Pallas kernels  62.4 us (94%)
  local copies, waits for them, and re-layouts  1.87 us (3%)
  other arithmetic  1.28 us (2%)
    pallas_call x1, Pallas kernels, body(): pl.pallas_call(functools.partial(kernel, NR, NX, NZ), out_shape=jax.Shape...  62.4 us
    unnamed x1, local copies, waits for them, and re-layouts  1.87 us

profile of v5, /device:TPU:0, one launch (start us, length us, event | category | flops | bytes accessed | tf_op | source)
XLA Modules:
  0.0 66.2 jit_solution(1609377937589377963)
XLA Ops:
  0.7 0.7 %compare_select_fusion = s32[24]{0:T(128)S(1)} fusion(s32[1,1,24]{2,1,0:T(1,128)} %param.7, s32[1,1,24]{2,1,0:T(1,128)} %param.6, s32[]{:T(128)} %bitcast.4), kind=kLoop, calls=%fused_computation.2 | loop fusion | flops 96 | bytes 292 | tf_op jit(solution)/shard_map/jit(_where)/select_n | solution.py:317
  1.3 0.6 select_reduce_fusion.table
  1.9 62.4 %shard_map.55 = f32[512,256]{1,0:T(8,128)} custom-call(s32[64]{0:T(128)} %select_reduce_fusion.table, bf16[512,256]{1,0:T(8,128)(2,1)} %basis.1, bf16[24,256,256]{2,1,0:T(8,128)(2,1)} %bitcast.5), custom_call_target="tpu_custom_call" | custom-call | tf_op jit(solution)/shard_map/pallas_call | solution.py:325
  64.3 1.9 %copy.8 = f32[512,256]{1,0:T(8,128)} copy(f32[512,256]{1,0:T(8,128)} %shard_map.55) | data formatting | bytes 1048576

commit v6 on v4

--- a/solution.py
+++ b/solution.py
@@ -182,8 +182,8 @@
             start(remote(ref, ref, az_ss.at[h, dz], a_sr.at[h, x * NZ + z], dev(y, k, t, x)))
         pass_x(h, z)
 
-    def spread(h):
-        for t in z_order:
+    def spread(h, order):
+        for t in order:
             await_recv(row_basis.at[h, p_rows(x, t)], a_sr.at[h, x * NZ + t])
             pass_x(h, t)
 
@@ -250,24 +250,28 @@
             lay_all()
         settle(h)
         if h > 0:
-            spread(h - 1)
+            spread(h - 1, z_order)
             back_own(h - 1)
     if chunks == 1:
         lay_all()
     last = chunks - 1
     reduce_z(last)
     if last > 0:
-        spread(last - 1)
+        spread(last - 1, z_order)
     settle(last)
     if last > 0:
         back_own(last - 1)
-    spread(last)
-    for h in range(chunks):
-        if h == last:
-            back_own(h)
+    spread(last, z_order[:1])
+    for h in range(last):
         collect(h)
         back_core(h)
+    spread(last, z_order[1:])
+    for h in range(last):
         back_y(h)
+    back_own(last)
+    collect(last)
+    back_core(last)
+    back_y(last)
     for h in range(chunks):
         finish(h)
     for copy in sends:

time: 64.9 us -> 63.8 us (0.983)
  Pallas kernels: 60.9 us -> 59.5 us
    pallas_call x1, Pallas kernels: 60.9 us -> 59.5 us  [body(): pl.pallas_call(functools.partial(kernel, NR, NX, NZ), out_shape=jax.Shape...]
where the time goes in v6:
time: 63.8 us; the launch traced here: 63.3 us
  Pallas kernels  59.5 us (93%)
  local copies, waits for them, and re-layouts  1.87 us (3%)
  other arithmetic  1.28 us (2%)
  between operations  0.66 us (1%)
    pallas_call x1, Pallas kernels, body(): pl.pallas_call(functools.partial(kernel, NR, NX, NZ), out_shape=jax.Shape...  59.5 us
    unnamed x1, local copies, waits for them, and re-layouts  1.87 us

profile of v6, /device:TPU:0, one launch (start us, length us, event | category | flops | bytes accessed | tf_op | source)
XLA Modules:
  0.0 63.3 jit_solution(9335921554077800446)
XLA Ops:
  0.7 0.7 %compare_select_fusion = s32[24]{0:T(128)S(1)} fusion(s32[1,1,24]{2,1,0:T(1,128)} %param.7, s32[1,1,24]{2,1,0:T(1,128)} %param.6, s32[]{:T(128)} %bitcast.4), kind=kLoop, calls=%fused_computation.2 | loop fusion | flops 96 | bytes 292 | tf_op jit(solution)/shard_map/jit(_where)/select_n | solution.py:292
  1.3 0.6 select_reduce_fusion.table
  1.9 59.5 %shard_map.55 = f32[512,256]{1,0:T(8,128)} custom-call(s32[64]{0:T(128)} %select_reduce_fusion.table, bf16[512,256]{1,0:T(8,128)(2,1)} %basis.1, bf16[24,256,256]{2,1,0:T(8,128)(2,1)} %bitcast.5), custom_call_target="tpu_custom_call" | custom-call | tf_op jit(solution)/shard_map/pallas_call | solution.py:300
  61.4 1.9 %copy.8 = f32[512,256]{1,0:T(8,128)} copy(f32[512,256]{1,0:T(8,128)} %shard_map.55) | data formatting | bytes 1048576

commit v7 on v6

--- a/solution.py
+++ b/solution.py
@@ -118,12 +118,12 @@
 
     lax.fori_loop(0, RB, lay, 0)
 
-    def turn_all():
+    def turn_some(first, last):
         def turn(s, _):
             turned[s] = held[s].T
             return 0
 
-        lax.fori_loop(0, slots + 1, turn, 0)
+        lax.fori_loop(first, last, turn, 0)
 
     def lay_all():
         def lay_turned(j, _):
@@ -234,7 +234,7 @@
             total = total + yr[h, dy].astype(jnp.float32)
         out[:, pl.ds(h * LANES, LANES)] = total
 
-    turn_all()
+    turn_some(0, slots // 2)
     for h in range(chunks):
         gather(h)
     for h in range(chunks):
@@ -247,12 +247,14 @@
     for h in range(chunks - 1):
         reduce_z(h)
         if h == 0:
+            turn_some(slots // 2, slots + 1)
             lay_all()
         settle(h)
         if h > 0:
             spread(h - 1, z_order)
             back_own(h - 1)
     if chunks == 1:
+        turn_some(slots // 2, slots + 1)
         lay_all()
     last = chunks - 1
     reduce_z(last)

time: 63.8 us -> 63.8 us (level)
  no operation moved by 1% of the time
where the time goes in v7:
time: 63.8 us; the launch traced here: 63.3 us
  Pallas kernels  59.5 us (93%)
  local copies, waits for them, and re-layouts  1.87 us (3%)
  other arithmetic  1.28 us (2%)
  between operations  0.66 us (1%)
    pallas_call x1, Pallas kernels, body(): pl.pallas_call(functools.partial(kernel, NR, NX, NZ), out_shape=jax.Shape...  59.5 us
    unnamed x1, local copies, waits for them, and re-layouts  1.87 us

profile of v7, /device:TPU:0, one launch (start us, length us, event | category | flops | bytes accessed | tf_op | source)
XLA Modules:
  0.0 63.3 jit_solution(10339322349177360227)
XLA Ops:
  0.7 0.7 %compare_select_fusion = s32[24]{0:T(128)S(1)} fusion(s32[1,1,24]{2,1,0:T(1,128)} %param.7, s32[1,1,24]{2,1,0:T(1,128)} %param.6, s32[]{:T(128)} %bitcast.4), kind=kLoop, calls=%fused_computation.2 | loop fusion | flops 96 | bytes 292 | tf_op jit(solution)/shard_map/jit(_where)/select_n | solution.py:294
  1.3 0.6 select_reduce_fusion.table
  1.9 59.5 %shard_map.55 = f32[512,256]{1,0:T(8,128)} custom-call(s32[64]{0:T(128)} %select_reduce_fusion.table, bf16[512,256]{1,0:T(8,128)(2,1)} %basis.1, bf16[24,256,256]{2,1,0:T(8,128)(2,1)} %bitcast.5), custom_call_target="tpu_custom_call" | custom-call | tf_op jit(solution)/shard_map/pallas_call | solution.py:302
  61.4 1.9 %copy.8 = f32[512,256]{1,0:T(8,128)} copy(f32[512,256]{1,0:T(8,128)} %shard_map.55) | data formatting | bytes 1048576
